TPU v7x, 512 devices: a whole 4x8x8 slice. The times are simulated.
512 devices in a mesh: comm: 64 (over x, y, core), blk: 8 (over z).
Axes of the slice: x: 4, y: 8, z: 8, core: 2. Of those that a mesh axis runs over, the one named last changes fastest.
Arguments:
- features: float32 [65536, 256], P(('comm', 'blk')), may hold values from -6 to 6
- tiles: float32 [65536, 1024], P(('comm', 'blk')), may hold values from -0.1875 to 0.1875
- weight: float32 [256, 256], replicated, may hold values from -0.375 to 0.375
- cotangent: float32 [65536, 256], P(('comm', 'blk')), may hold values from -6 to 6
- send_count: int32 [512, 64], P(('comm', 'blk')), may hold values from 0 to 16, as said below
- send_index: int32 [512, 1024], P(('comm', 'blk')), may hold values from 0 to 127
- cross_dst: int32 [512, 1024], P(('comm', 'blk')), may hold values from 0 to 127
- cross_weight: float32 [512, 1024], P(('comm', 'blk')), may hold values from -2.4 to 2.4
Outputs:
- output: float32 [65536, 256], P(('comm', 'blk'))
- grad_features: float32 [65536, 256], P(('comm', 'blk'))
- grad_weight: float32 [256, 256], replicated
Inputs may be any that keep to these rules, and one draw needn't show every extreme that they name: send_count[d, p] is 0 where p is d's own community and at least 1 elsewhere; every device sends exactly 16 rows to some other community.
All inputs are finite; a program needn't handle non-finite values.
Results may differ from a plain program's by a relative error of at most 0.0003.
Values sent between devices are 32-bit elements; how exact they have to be, the bound alone decides.
A program may use at most 64 MiB of HBM per device.

v0:
```python
import jax
import jax.numpy as jnp
from jax import lax
from jax.sharding import PartitionSpec as P


def body(features, tiles, weight, cotangent, send_count, send_index, cross_dst, cross_weight):
    rows, width = features.shape
    groups = lax.axis_size("comm")
    blocks = lax.axis_size("blk")
    slot_total = send_index.shape[1]
    per_peer = slot_total // groups
    counts = send_count[0]
    index = send_index[0].reshape(groups, per_peer)
    valid = (jnp.arange(per_peer, dtype=jnp.int32)[None, :] < counts[:, None]).astype(jnp.float32)
    targets = cross_dst[0]
    edge_weight = cross_weight[0]
    highest = lax.Precision.HIGHEST
    outgoing = features[index] * valid[:, :, None]
    incoming = lax.all_to_all(outgoing, "comm", split_axis=0, concat_axis=0, tiled=True).reshape(
        slot_total, width
    )
    columns = tiles
    local = jnp.dot(columns, lax.all_gather(features, "blk", axis=0, tiled=True), precision=highest)
    cross = jax.ops.segment_sum(edge_weight[:, None] * incoming, targets, num_segments=rows)
    aggregated = local + cross
    pre = jnp.dot(aggregated, weight, precision=highest)
    output, pull = jax.vjp(lambda value: jax.nn.gelu(value, approximate=False), pre)
    grad_pre = pull(cotangent)[0]
    partial_weight = lax.dot_general(
        aggregated, grad_pre, (((0,), (0,)), ((), ())), precision=highest
    )
    nodes = rows * groups * blocks
    grad_weight = lax.psum(partial_weight, ("comm", "blk")) * nodes ** (-0.5)
    spread = jnp.dot(grad_pre, weight.T, precision=highest)
    columns = tiles
    inner_grad = lax.psum_scatter(
        lax.dot_general(columns, spread, (((0,), (0,)), ((), ())), precision=highest),
        "blk",
        scatter_dimension=0,
        tiled=True,
    )
    slot_grads = (edge_weight[:, None] * spread[targets]).reshape(groups, per_peer, width)
    returned = lax.all_to_all(slot_grads, "comm", split_axis=0, concat_axis=0, tiled=True)
    returned = (returned * valid[:, :, None]).reshape(slot_total, width)
    boundary_grad = jax.ops.segment_sum(returned, index.reshape(slot_total), num_segments=rows)
    return (output, inner_grad + boundary_grad, grad_weight)


def solution(mesh):
    return jax.shard_map(
        body,
        mesh=mesh,
        in_specs=(
            P(("comm", "blk"), None),
            P(("comm", "blk"), None),
            P(),
            P(("comm", "blk"), None),
            P(("comm", "blk"), None),
            P(("comm", "blk"), None),
            P(("comm", "blk"), None),
            P(("comm", "blk"), None),
        ),
        out_specs=(P(("comm", "blk"), None), P(("comm", "blk"), None), P()),
        check_vma=False,
    )
```

profile of v0, /device:TPU:1, one launch (start us, length us, event | category | flops | bytes accessed | tf_op | source)
XLA Modules:
  0.0 389.0 jit_solution(13132864459862080170)
XLA Ops:
  7.2 0.0 copy-start
  7.2 0.0 copy-start.1
  7.2 0.0 all-gather.2.cloned.1.call-start
  7.2 0.7 all-gather.2.cloned.1.call-update
  7.9 0.5 broadcast.83
  8.4 1.3 reduce.6
  9.8 0.1 reshape_squeeze.3
  9.9 0.1 reshape.105
  10.0 0.0 copy-start.8
  10.0 0.6 copy-done.8
  10.6 0.1 fusion.6
  10.7 3.5 gather_fusion
  14.2 1.2 broadcast_multiply_fusion.2
  15.4 11.8 %all-to-all-start = ((f32[64,16,256]{2,1,0:T(8,128)}), f32[64,16,256]{2,1,0:T(8,128)S(1)}, u32[]{:S(2)}, u32[]{:S(2)}) async-start(f32[64,16,256]{2,1,0:T(8,128)} %broadcast_multiply_fusion.2), calls=%async_computation | async-start | bytes 2097152 | tf_op jit(solution)/shard_map/all_to_all | solution.py:20
  27.2 0.0 all-reduce.2.cloned.1.call-start
  27.2 0.5 broadcast.84
  27.7 0.0 copy-done.5
  27.7 0.7 reduce.7
  28.4 0.0 copy-start.6
  28.4 0.1 mul.86
  28.5 0.6 copy-done.6
  29.1 24.3 %all-gather.2.cloned.1.call-done = f32[1024,256]{1,0:T(8,128)} async-done(((f32[128,256]{1,0:T(8,128)}), f32[1024,256]{1,0:T(8,128)}) %all-gather.2.cloned.1.call-update) | async-done | bytes 1048592 | tf_op jit(solution)/shard_map/all_gather | solution.py:24
  53.4 1.9 fusion.10
  55.2 0.5 all-to-all-done
  55.7 0.2 bitcast_multiply_fusion
  55.9 0.0 copy-start.4
  55.9 6.1 %scatter_fusion = f32[128,256]{1,0:T(8,128)S(1)} fusion(f32[128,256]{1,0:T(8,128)S(1)} %fusion.10, s32[1024]{0:T(1024)S(1)} %bitcast.28, f32[1024,256]{1,0:T(8,128)S(1)} %bitcast_multiply_fusion), kind=kCustom, calls=%fused_computation.2 | custom fusion | flops 262144 | bytes 3149824 | tf_op jit(solution)/shard_map/scatter-add | solution.py:25
  62.1 0.0 copy-done.4
  62.1 0.0 copy-start.3
  62.1 1.2 multiply_multiply_fusion.5
  63.3 0.4 fusion.8
  63.7 1.1 fusion.7
  64.8 0.0 all-reduce.2.cloned.1.call-update
  64.8 3.5 gather_fusion.1
  68.3 1.2 broadcast_multiply_fusion
  69.5 14.2 %all-to-all-start.1 = ((f32[64,16,256]{2,1,0:T(8,128)}), f32[64,16,256]{2,1,0:T(8,128)S(1)}, u32[]{:S(2)}, u32[]{:S(2)}) async-start(f32[64,16,256]{2,1,0:T(8,128)} %broadcast_multiply_fusion), calls=%async_computation.2 | async-start | bytes 2097152 | tf_op jit(solution)/shard_map/all_to_all | solution.py:44
  83.7 0.0 reduce-scatter.2.cloned.1.call-start
  83.8 2.0 convolution_bitcast_fusion
  85.8 0.0 reduce-scatter.2.cloned.1.call-update
  85.8 252.4 %all-reduce.2.cloned.1.call-done = f32[256,256]{1,0:T(8,128)} async-done(((f32[256,256]{1,0:T(8,128)}), f32[256,256]{1,0:T(8,128)}) %all-reduce.2.cloned.1.call-update) | async-done | bytes 262160 | tf_op jit(solution)/shard_map/psum | solution.py:34
  338.2 1.7 broadcast_multiply_fusion.3
  339.9 0.0 all-to-all-done.1
  339.9 0.2 broadcast_multiply_fusion.1
  340.1 34.5 %reduce-scatter.2.cloned.1.call-done = f32[128,256]{0,1:T(8,128)} async-done(((f32[1024,256]{0,1:T(8,128)}), f32[128,256]{0,1:T(8,128)}) %reduce-scatter.2.cloned.1.call-update) | async-done | bytes 131088 | tf_op jit(solution)/shard_map/reduce_scatter | solution.py:37
  374.6 1.0 copy.12
  375.7 6.1 %scatter_fusion.1 = f32[128,256]{1,0:T(8,128)S(1)} fusion(f32[128,256]{1,0:T(8,128)S(1)} %copy.12, s32[1024]{0:T(1024)S(1)} %bitcast.29, f32[1024,256]{1,0:T(8,128)S(1)} %bitcast.24), kind=kCustom, calls=%fused_computation.3 | custom fusion | flops 262144 | bytes 3149824 | tf_op jit(solution)/shard_map/scatter-add | solution.py:46
  381.8 0.0 copy-start.2
  381.8 0.6 copy-done.2
  (10 shorter events, 0.0 us)
Async XLA Ops:
  7.2 46.2 %copy-start = (f32[128,1024]{1,0:T(8,128)S(1)}, f32[128,1024]{1,0:T(8,128)}, u32[]{:S(2)}) copy-start(f32[128,1024]{1,0:T(8,128)} %param.9) | copy-start | bytes 1572868
  7.2 3.5 copy-start.1
  7.2 46.2 %all-gather.2.cloned.1.call-start = ((), (), s32[]{:S(2)}) async-start(), calls=%async_computation.3 | async-start | bytes 1179648 | tf_op jit(solution)/shard_map/all_gather | solution.py:24
  10.0 0.7 copy-start.8
  15.4 12.3 %copy-start.5 = (f32[1,1024]{1,0:T(1,128)S(1)}, f32[1,1024]{1,0:T(1,128)}, u32[]{:S(2)}) copy-start(f32[1,1024]{1,0:T(1,128)} %param.15) | copy-start | bytes 12292
  15.4 40.3 %all-to-all-start = ((f32[64,16,256]{2,1,0:T(8,128)}), f32[64,16,256]{2,1,0:T(8,128)S(1)}, u32[]{:S(2)}, u32[]{:S(2)}) async-start(f32[64,16,256]{2,1,0:T(8,128)} %broadcast_multiply_fusion.2), calls=%async_computation | async-start | bytes 2097152 | tf_op jit(solution)/shard_map/all_to_all | solution.py:20
  27.2 311.1 %all-reduce.2.cloned.1.call-start = ((), (), s32[]{:S(2)}) async-start(), calls=%async_computation.5 | async-start | bytes 524288 | tf_op jit(solution)/shard_map/psum | solution.py:34
  28.4 0.7 copy-start.6
  55.9 6.2 %copy-start.4 = (f32[256,256]{1,0:T(8,128)S(1)}, f32[256,256]{1,0:T(8,128)}, u32[]{:S(2)}) copy-start(f32[256,256]{1,0:T(8,128)} %param.10) | copy-start | bytes 786436
  62.1 1.2 copy-start.3
  69.5 270.4 %all-to-all-start.1 = ((f32[64,16,256]{2,1,0:T(8,128)}), f32[64,16,256]{2,1,0:T(8,128)S(1)}, u32[]{:S(2)}, u32[]{:S(2)}) async-start(f32[64,16,256]{2,1,0:T(8,128)} %broadcast_multiply_fusion), calls=%async_computation.2 | async-start | bytes 2097152 | tf_op jit(solution)/shard_map/all_to_all | solution.py:44
  83.7 290.9 %reduce-scatter.2.cloned.1.call-start = ((), (), s32[]{:S(2)}) async-start(), calls=%async_computation.4 | async-start | bytes 1179648 | tf_op jit(solution)/shard_map/reduce_scatter | solution.py:37
  374.6 1.0 copy-start.7
  381.8 0.7 copy-start.2
Sparse Core Ops, SparseCore 0:
  10.1 43.2 all-gather.1
  65.0 273.2 all-reduce.1
  341.3 33.2 reduce-scatter.1
where the time goes:
time: 394 us; the launch traced here: 389 us
  waiting for transfers between devices  312 us (79%)
  starting transfers between devices  26 us (7%)
  other arithmetic  18.9 us (5%)
  between operations  13.9 us (4%)
  local copies, waits for them, and re-layouts  11.1 us (3%)
  matrix products  6.58 us (2%)
    psum x1, waiting for transfers between devices, body(): grad_weight = lax.psum(partial_weight, ('comm', 'blk')) * nodes ** (-0.5)  252 us
    reduce_scatter x1, waiting for transfers between devices, body(): lax.psum_scatter(lax.dot_general(columns, spread, (((0,), (0,)), ((), ())...  34.5 us
    all_gather x1, waiting for transfers between devices, body(): lax.all_gather(features, 'blk', axis=0, tiled=True)  24.3 us
    all_to_all x1, starting transfers between devices, body(): lax.all_to_all(slot_grads, 'comm', split_axis=0, concat_axis=0, tiled=True)  14.2 us
    all_to_all x1, starting transfers between devices, body(): lax.all_to_all(outgoing, 'comm', split_axis=0, concat_axis=0, tiled=True)  11.8 us
  transfers between devices with their start and end apart: 5, of which 4 were waited for; matrix products, arithmetic and copies ran while one was open for 5% of the time, Pallas kernels for 0%

commit v1 on v0

v1 whole, which is shorter than its diff:
```python
import functools

import jax
import jax.numpy as jnp
from jax import lax
from jax.experimental import pallas as pl
from jax.experimental.pallas import tpu as pltpu
from jax.sharding import PartitionSpec as P

MESH = pl.DeviceIdType.MESH
F32 = jnp.float32
BF16 = jnp.bfloat16


def split(x):
    hi = x.astype(BF16)
    lo = (x - hi.astype(F32)).astype(BF16)
    return hi, lo


def mm(a, b, ca=1, cb=0):
    return lax.dot_general(a, b, (((ca,), (cb,)), ((), ())), preferred_element_type=F32)


def mm3(a, b, ca=1, cb=0):
    return mm(a[0], b[0], ca, cb) + (mm(a[0], b[1], ca, cb) + mm(a[1], b[0], ca, cb))


def kernel(
    groups, blocks, ny,
    f_ref, t_ref, w_ref, ct_ref, cnt_ref, idx_ref, dst_ref, cw_ref,
    out_ref, gf_ref, gw_ref,
    send_buf, recv_buf, gath, send2_buf, recv2_buf, part, part_in,
    wpart, wz, wa, wy, wfin, wall, wsum,
    sems,
):
    rows, width = f_ref.shape
    slots = idx_ref.shape[1]
    cap = slots // groups
    me_c = lax.axis_index("comm")
    me_b = lax.axis_index("blk")
    na = groups // ny
    core = lax.rem(me_c, 2)
    my_y = lax.rem(me_c // 2, ny)
    my_x = me_c // (2 * ny)
    my_a = my_x * 2 + core

    def a_peer(a):
        return ((a // 2) * ny + my_y) * 2 + lax.rem(a, 2)

    def y_peer(y):
        return (my_x * ny + y) * 2 + core

    barrier = pltpu.get_barrier_semaphore()

    @pl.loop(1, groups)
    def _(i):
        pl.semaphore_signal(barrier, inc=1, device_id=(lax.rem(me_c + i, groups), me_b), device_id_type=MESH)

    @pl.loop(1, blocks)
    def _(i):
        pl.semaphore_signal(barrier, inc=1, device_id=(me_c, lax.rem(me_b + i, blocks)), device_id_type=MESH)

    spot = lax.broadcasted_iota(jnp.int32, (groups, slots), 1) // cap
    peer = lax.broadcasted_iota(jnp.int32, (groups, slots), 0)
    expand = (spot == peer).astype(BF16)
    counts = jnp.broadcast_to(cnt_ref[...].astype(F32).astype(BF16), (16, groups))
    count = mm(counts, expand)[0:1, :]
    place = lax.rem(lax.broadcasted_iota(jnp.int32, (1, slots), 1), cap).astype(F32)
    index = jnp.where(place < count, idx_ref[...], -1)
    node = lax.broadcasted_iota(jnp.int32, (rows, slots), 0)
    pick = (node == index).astype(BF16)
    f = f_ref[...]
    f2 = split(f)
    send_buf[...] = mm(pick, f2[0], 0, 0) + mm(pick, f2[1], 0, 0)
    gath[pl.ds(pl.multiple_of(me_b * rows, rows), rows), :] = f
    own = pl.ds(pl.multiple_of(me_c * cap, cap), cap)
    recv_buf[own, :] = jnp.zeros((cap, width), F32)
    recv2_buf[own, :] = jnp.zeros((cap, width), F32)

    pl.semaphore_wait(barrier, groups + blocks - 2)

    def spread_comm(src, dst, s, r):
        @pl.loop(1, groups)
        def _(i):
            p = lax.rem(me_c + i, groups)
            pltpu.make_async_remote_copy(
                src_ref=src.at[pl.ds(pl.multiple_of(p * cap, cap), cap)],
                dst_ref=dst.at[own],
                send_sem=sems.at[s], recv_sem=sems.at[r],
                device_id=(p, me_b), device_id_type=MESH,
            ).start()

    def wait_bytes(ref, n, s):
        pltpu.make_async_copy(ref.at[pl.ds(0, n)], ref.at[pl.ds(0, n)], sems.at[s]).wait()

    @pl.loop(1, blocks)
    def _(i):
        pltpu.make_async_remote_copy(
            src_ref=f_ref,
            dst_ref=gath.at[pl.ds(pl.multiple_of(me_b * rows, rows), rows)],
            send_sem=sems.at[0], recv_sem=sems.at[1],
            device_id=(me_c, lax.rem(me_b + i, blocks)), device_id_type=MESH,
        ).start()

    spread_comm(send_buf, recv_buf, 2, 3)

    t2 = split(t_ref[...])
    feeds = node == dst_ref[...]
    cw2 = split(cw_ref[...])
    s2 = tuple(jnp.where(feeds, jnp.broadcast_to(c.astype(F32), (rows, slots)), 0.0).astype(BF16) for c in cw2)
    w2 = split(w_ref[...])

    wait_bytes(gath, rows * (blocks - 1), 1)
    agg = mm3(t2, split(gath[...]))
    wait_bytes(recv_buf, cap * (groups - 1), 3)
    agg = agg + mm3(s2, split(recv_buf[...]))
    agg2 = split(agg)
    pre = mm3(agg2, w2)
    cdf = 0.5 * (1.0 + lax.erf(pre * 0.7071067811865476))
    out_ref[...] = pre * cdf
    slope = cdf + pre * (jnp.exp(-0.5 * pre * pre) * 0.3989422804014327)
    gp = ct_ref[...] * slope
    gp2 = split(gp)
    wpart[...] = mm3(agg2, gp2, 0, 0)

    wrows = wpart.shape[0] // blocks

    @pl.loop(1, blocks)
    def _(i):
        j = lax.rem(me_b + i, blocks)
        pltpu.make_async_remote_copy(
            src_ref=wpart.at[pl.ds(pl.multiple_of(j * wrows, wrows), wrows)],
            dst_ref=wz.at[me_b],
            send_sem=sems.at[4], recv_sem=sems.at[5],
            device_id=(me_c, j), device_id_type=MESH,
        ).start()

    spread = mm3(gp2, w2, 1, 1)
    sp2 = split(spread)
    send2_buf[...] = mm3(s2, sp2, 0, 0)
    spread_comm(send2_buf, recv2_buf, 6, 7)
    part[...] = mm3(t2, sp2, 0, 0)

    @pl.loop(1, blocks)
    def _(i):
        j = lax.rem(me_b + i, blocks)
        pltpu.make_async_remote_copy(
            src_ref=part.at[pl.ds(pl.multiple_of(j * rows, rows), rows)],
            dst_ref=part_in.at[me_b],
            send_sem=sems.at[8], recv_sem=sems.at[9],
            device_id=(me_c, j), device_id_type=MESH,
        ).start()

    part_in[me_b] = part[pl.ds(pl.multiple_of(me_b * rows, rows), rows), :]

    wz[me_b] = wpart[pl.ds(pl.multiple_of(me_b * wrows, wrows), wrows), :]
    wait_bytes(wz, blocks - 1, 5)
    mine = jnp.sum(wz[...], axis=0)
    half = width // 2
    piece = 2 * wrows // na
    wsum[0:wrows, :] = mine[:, :half]
    wsum[wrows:, :] = mine[:, half:]

    @pl.loop(1, na)
    def _(i):
        a = lax.rem(my_a + i, na)
        pltpu.make_async_remote_copy(
            src_ref=wsum.at[pl.ds(pl.multiple_of(a * piece, piece), piece)],
            dst_ref=wa.at[my_a],
            send_sem=sems.at[10], recv_sem=sems.at[11],
            device_id=(a_peer(a), me_b), device_id_type=MESH,
        ).start()

    wa[my_a] = wsum[pl.ds(pl.multiple_of(my_a * piece, piece), piece), :]
    wait_bytes(wa, na - 1, 11)
    wy[my_y] = jnp.sum(wa[...], axis=0)

    @pl.loop(1, ny)
    def _(i):
        y = lax.rem(my_y + i, ny)
        pltpu.make_async_remote_copy(
            src_ref=wy.at[my_y],
            dst_ref=wy.at[my_y],
            send_sem=sems.at[12], recv_sem=sems.at[13],
            device_id=(y_peer(y), me_b), device_id_type=MESH,
        ).start()

    wait_bytes(wy, ny - 1, 13)
    nodes = rows * groups * blocks
    wfin[my_a] = jnp.sum(wy[...], axis=0) * nodes ** (-0.5)

    @pl.loop(1, na)
    def _(i):
        a = lax.rem(my_a + i, na)
        pltpu.make_async_remote_copy(
            src_ref=wfin.at[my_a],
            dst_ref=wfin.at[my_a],
            send_sem=sems.at[14], recv_sem=sems.at[15],
            device_id=(a_peer(a), me_b), device_id_type=MESH,
        ).start()

    wait_bytes(wfin, na - 1, 15)
    wall[me_b] = wfin[...].reshape(na * piece, half)

    @pl.loop(1, blocks)
    def _(i):
        j = lax.rem(me_b + i, blocks)
        pltpu.make_async_remote_copy(
            src_ref=wall.at[me_b],
            dst_ref=wall.at[me_b],
            send_sem=sems.at[16], recv_sem=sems.at[17],
            device_id=(me_c, j), device_id_type=MESH,
        ).start()

    wait_bytes(part_in, blocks - 1, 9)
    inner = jnp.sum(part_in[...], axis=0)
    wait_bytes(recv2_buf, cap * (groups - 1), 7)
    back2 = split(recv2_buf[...])
    gf_ref[...] = inner + (mm(pick, back2[0]) + mm(pick, back2[1]))

    wait_bytes(wall, blocks - 1, 17)
    for j in range(blocks):
        gw_ref[j * wrows:(j + 1) * wrows, :half] = wall[j, 0:wrows, :]
        gw_ref[j * wrows:(j + 1) * wrows, half:] = wall[j, wrows:, :]

    wait_bytes(gath, rows * (blocks - 1), 0)
    wait_bytes(recv_buf, cap * (groups - 1), 2)
    wait_bytes(wz, blocks - 1, 4)
    wait_bytes(recv2_buf, cap * (groups - 1), 6)
    wait_bytes(part_in, blocks - 1, 8)
    wait_bytes(wa, na - 1, 10)
    wait_bytes(wy, ny - 1, 12)
    wait_bytes(wfin, na - 1, 14)
    wait_bytes(wall, blocks - 1, 16)


def body(features, tiles, weight, cotangent, send_count, send_index, cross_dst, cross_weight):
    rows, width = features.shape
    groups = lax.axis_size("comm")
    blocks = lax.axis_size("blk")
    slots = send_index.shape[1]
    ny = 8
    na = groups // ny
    wrows = width // blocks
    piece = 2 * wrows // na
    half = width // 2
    vmem = pltpu.VMEM
    return pl.pallas_call(
        functools.partial(kernel, groups, blocks, ny),
        out_shape=(
            jax.ShapeDtypeStruct((rows, width), F32),
            jax.ShapeDtypeStruct((rows, width), F32),
            jax.ShapeDtypeStruct((width, width), F32),
        ),
        in_specs=[pl.BlockSpec(memory_space=vmem)] * 8,
        out_specs=(pl.BlockSpec(memory_space=vmem),) * 3,
        scratch_shapes=[
            vmem((slots, width), F32),
            vmem((slots, width), F32),
            vmem((blocks * rows, width), F32),
            vmem((slots, width), F32),
            vmem((slots, width), F32),
            vmem((blocks * rows, width), F32),
            vmem((blocks, rows, width), F32),
            vmem((width, width), F32),
            vmem((blocks, wrows, width), F32),
            vmem((na, piece, half), F32),
            vmem((ny, piece, half), F32),
            vmem((na, piece, half), F32),
            vmem((blocks, 2 * wrows, half), F32),
            vmem((2 * wrows, half), F32),
            pltpu.SemaphoreType.DMA((18,)),
        ],
        compiler_params=pltpu.CompilerParams(
            collective_id=0, has_side_effects=True, vmem_limit_bytes=40 * 1024 * 1024
        ),
    )(features, tiles, weight, cotangent, send_count, send_index, cross_dst, cross_weight)


def solution(mesh):
    rows = P(("comm", "blk"), None)
    return jax.shard_map(
        body,
        mesh=mesh,
        in_specs=(rows, rows, P(), rows, rows, rows, rows, rows),
        out_specs=(rows, rows, P()),
        check_vma=False,
    )
```

time: 394 us -> 91.9 us (0.23); the launches traced: 389 us -> 91.5 us
  waiting for transfers between devices: 312 us -> 0 us
  Pallas kernels: 0 us -> 82.3 us
  starting transfers between devices: 26 us -> 0 us
  other arithmetic: 18.9 us -> 0 us
  between operations: 13.9 us -> 0.66 us
  matrix products: 6.58 us -> 0 us
    psum x1 -> x0, waiting for transfers between devices: 252 us -> none  [body(): grad_weight = lax.psum(partial_weight, ('comm', 'blk')) * nodes ** (-0.5)]
    pallas_call x0 -> x1, Pallas kernels: none -> 82.3 us  [body(): pl.pallas_call(functools.partial(kernel, groups, blocks, ny), out_shape=(...]
    reduce_scatter x1 -> x0, waiting for transfers between devices: 34.5 us -> none  [body(): lax.psum_scatter(lax.dot_general(columns, spread, (((0,), (0,)), ((), ())...]
    all_to_all x2 -> x0, starting transfers between devices: 25.9 us -> none  [the longest x1 14.2 us: body(): lax.all_to_all(slot_grads, 'comm', split_axis=0, concat_axis=0, tiled=True)]
    all_gather x1 -> x0, waiting for transfers between devices: 24.3 us -> none  [body(): lax.all_gather(features, 'blk', axis=0, tiled=True)]
    scatter-add x2 -> x0, other arithmetic: 12.3 us -> none  [the longest x1 6.13 us: body(): jax.ops.segment_sum(edge_weight[:, None] * incoming, targets, num_segment...]
    gather x2 -> x0, local copies, waits for them, and re-layouts: 6.93 us -> none  [the longest x1 3.47 us: body(): spread[targets]]
    dot_general x5 -> x0, matrix products: 6.58 us -> none  [the longest x1 2.01 us: body(): lax.dot_general(columns, spread, (((0,), (0,)), ((), ())), precision=high...]
  transfers between devices with their start and end apart: 5 -> 0, of which waited for: 4 -> 0; matrix products, arithmetic and copies ran while one was open for 5% -> 0% of each run, Pallas kernels for 0% -> 0%
where the time goes in v1:
time: 91.9 us; the launch traced here: 91.5 us
  Pallas kernels  82.3 us (90%)
  local copies, waits for them, and re-layouts  8.52 us (9%)
    pallas_call x1, Pallas kernels, body(): pl.pallas_call(functools.partial(kernel, groups, blocks, ny), out_shape=(...  82.3 us
    unnamed x19, local copies, waits for them, and re-layouts  8.52 us

profile of v1, /device:TPU:1, one launch (start us, length us, event | category | flops | bytes accessed | tf_op | source)
XLA Modules:
  0.0 91.5 jit_solution(7874118273370476463)
XLA Ops:
  0.6 0.0 copy-start
  0.6 1.0 %copy-done = f32[128,1024]{1,0:T(8,128)S(1)} copy-done((f32[128,1024]{1,0:T(8,128)S(1)}, f32[128,1024]{1,0:T(8,128)}, u32[]{:S(2)}) %copy-start) | copy-done | bytes 524312
  1.7 0.0 copy-start.1
  1.7 0.9 %copy-done.1 = f32[256,256]{1,0:T(8,128)S(1)} copy-done((f32[256,256]{1,0:T(8,128)S(1)}, f32[256,256]{1,0:T(8,128)}, u32[]{:S(2)}) %copy-start.1) | copy-done | bytes 262168
  2.6 0.0 copy-start.2
  2.6 0.9 copy-done.2
  3.5 0.0 copy-start.3
  3.5 0.9 copy-done.3
  4.4 0.0 copy-start.4
  4.4 0.7 copy-done.4
  5.1 0.0 copy-start.5
  5.1 0.7 copy-done.5
  5.8 0.0 copy-start.6
  5.8 0.7 copy-done.6
  6.5 0.0 copy-start.7
  6.5 0.7 copy-done.7
  7.2 82.3 %shard_map.103 = (f32[128,256]{1,0:T(8,128)S(1)}, f32[128,256]{1,0:T(8,128)S(1)}, f32[256,256]{1,0:T(8,128)S(1)}) custom-call(f32[128,256]{1,0:T(8,128)S(1)} %copy-done.2, f32[128,1024]{1,0:T(8,128)S(1)} %copy-done, f32[256,256]{1,0:T(8,128)S(1)} %copy-done.1, f32[128,256]{1,0:T(8,128)S(1)} %copy-done.3, s32[1,64]{1,0:T(1,128)S(1)} %copy-done.7, ...), custom_call_target="tpu_custom_call" | custom-call | tf_op jit(solution)/shard_map/pallas_call | solution.py:249
  89.5 0.7 copy.14
  90.1 0.7 copy.15
  90.8 0.7 copy.16
Async XLA Ops:
  0.6 1.0 %copy-start = (f32[128,1024]{1,0:T(8,128)S(1)}, f32[128,1024]{1,0:T(8,128)}, u32[]{:S(2)}) copy-start(f32[128,1024]{1,0:T(8,128)} %t_ref.1) | copy-start | bytes 1572868
  1.7 0.9 %copy-start.1 = (f32[256,256]{1,0:T(8,128)S(1)}, f32[256,256]{1,0:T(8,128)}, u32[]{:S(2)}) copy-start(f32[256,256]{1,0:T(8,128)} %w_ref.1) | copy-start | bytes 786436
  2.6 0.9 copy-start.2
  3.5 0.9 copy-start.3
  4.4 0.7 copy-start.4
  5.1 0.7 copy-start.5
  5.8 0.7 copy-start.6
  6.5 0.7 copy-start.7

commit v2 on v0

v2 whole, which is shorter than its diff:
```python
import functools

import jax
import jax.numpy as jnp
from jax import lax
from jax.experimental import pallas as pl
from jax.experimental.pallas import tpu as pltpu
from jax.sharding import PartitionSpec as P

MESH = pl.DeviceIdType.MESH
F32 = jnp.float32
BF16 = jnp.bfloat16
NY = 8


def split(x):
    hi = x.astype(BF16)
    lo = (x - hi.astype(F32)).astype(BF16)
    return hi, lo


def mm(a, b, ca=1, cb=0):
    return lax.dot_general(a, b, (((ca,), (cb,)), ((), ())), preferred_element_type=F32)


def mm3(a, b, ca=1, cb=0):
    return mm(a[0], b[0], ca, cb) + (mm(a[0], b[1], ca, cb) + mm(a[1], b[0], ca, cb))


def at(i, n):
    return pl.ds(pl.multiple_of(i * n, n), n)


def kernel(
    groups, blocks,
    f_hbm, t_hbm, w_hbm, ct_hbm, cnt_hbm, idx_hbm, dst_hbm, cw_hbm,
    out_ref, gf_ref, gw_ref,
    t_ref, w_ref, ct_ref, cnt_ref, idx_ref, dst_ref, cw_ref,
    gath, picks, th, tl, idx_out, idx_in,
    send_buf, recv_buf, send2_buf, recv2_buf, part, rs_out, rs_in,
    wpart, wz, wa, wy, wfin, wall, wsum,
    loc, ag_r, ag_s, rs_r, rs_s, row_r, sems,
):
    rows, width = f_hbm.shape
    slots = idx_ref.shape[1]
    cap = slots // groups
    na = groups // NY
    unit = rows // 2
    me_c = lax.axis_index("comm")
    me_b = lax.axis_index("blk")
    core = lax.rem(me_c, 2)
    my_y = lax.rem(me_c // 2, NY)
    my_x = me_c // (2 * NY)
    my_a = my_x * 2 + core

    def a_dev(a):
        return (((a // 2) * NY + my_y) * 2 + lax.rem(a, 2), me_b)

    def y_dev(y):
        return ((my_x * NY + y) * 2 + core, me_b)

    def z_dev(z):
        return (me_c, z)

    ring = ((my_y, y_dev), (me_b, z_dev))
    n = NY

    def turn(r, d):
        return lax.rem(ring[r][0] + d + n, n)

    def send(src, dst, s, r, dev):
        pltpu.make_async_remote_copy(
            src_ref=src, dst_ref=dst, send_sem=s, recv_sem=r,
            device_id=dev, device_id_type=MESH,
        ).start()

    def wait_bytes(ref, s):
        pltpu.make_async_copy(ref, ref, s).wait()

    loads = [
        pltpu.make_async_copy(src, dst, loc.at[i])
        for i, (src, dst) in enumerate((
            (idx_hbm, idx_ref), (cnt_hbm, cnt_ref),
            (f_hbm, gath.at[0, at(my_y, rows)]), (f_hbm, gath.at[1, at(me_b, rows)]),
            (t_hbm, t_ref), (dst_hbm, dst_ref), (cw_hbm, cw_ref), (w_hbm, w_ref), (ct_hbm, ct_ref),
        ))
    ]
    for c in loads:
        c.start()

    barrier = pltpu.get_barrier_semaphore()

    @pl.loop(1, n)
    def _(i):
        pl.semaphore_signal(barrier, inc=1, device_id=y_dev(turn(0, i)), device_id_type=MESH)
        pl.semaphore_signal(barrier, inc=1, device_id=z_dev(turn(1, i)), device_id_type=MESH)
        pl.semaphore_signal(barrier, inc=1, device_id=a_dev(lax.rem(my_a + i, na)), device_id_type=MESH)

    per = na * cap
    spot = lax.broadcasted_iota(jnp.int32, (groups, slots), 1) // cap
    peer = lax.broadcasted_iota(jnp.int32, (groups, slots), 0)
    expand = (spot == peer).astype(BF16)
    lane = lax.broadcasted_iota(jnp.int32, (16, slots), 1)
    row16 = lax.broadcasted_iota(jnp.int32, (16, slots), 0)
    here = (lane // (2 * cap)) % NY == row16
    source = lax.broadcasted_iota(jnp.int32, (slots, per), 0)
    target = lax.broadcasted_iota(jnp.int32, (slots, per), 1)
    gather_lane = ((source // (2 * cap * NY)) * (2 * cap) + source % (2 * cap) == target).astype(BF16)
    loads[0].wait()
    loads[1].wait()
    counts = jnp.broadcast_to(cnt_ref[...].astype(F32).astype(BF16), (16, groups))
    count = mm(counts, expand)
    place = lax.rem(lane, cap).astype(F32)
    index = jnp.where(place < count, jnp.broadcast_to(idx_ref[...], (16, slots)).astype(F32), -1.0)
    mine = mm(jnp.where(here, index, 0.0).astype(BF16), gather_lane)
    for y in range(NY):
        idx_out[y] = jnp.broadcast_to(mine[y:y + 1, :], (8, per))
    idx_in[my_y] = idx_out[my_y]
    loads[2].wait()
    loads[3].wait()

    pl.semaphore_wait(barrier, 3 * (n - 1))

    def ag_slice(r, sign, u, origin):
        half = (u % 2) if sign > 0 else (1 - u % 2)
        return gath.at[r, pl.ds(pl.multiple_of(origin * rows + half * unit, unit), unit)]

    def ag_send(r, sign, u):
        origin = turn(r, -sign * (u // 2))
        s = ag_slice(r, sign, u, origin)
        k = 0 if sign > 0 else 1
        send(s, s, ag_s.at[2 * r + k], ag_r.at[(2 * r + k) * 7 + u], ring[r][1](turn(r, sign)))

    def ag_wait(r, sign, u):
        s = ag_slice(r, sign, u, turn(r, -sign * (u // 2 + 1)))
        k = 0 if sign > 0 else 1
        wait_bytes(s, ag_r.at[(2 * r + k) * 7 + u])

    @pl.loop(1, n)
    def _(i):
        y = turn(0, i)
        send(idx_out.at[y], idx_in.at[my_y], sems.at[0], sems.at[1], y_dev(y))

    for u in (0, 1):
        for r in (0, 1):
            for sign in (1, -1):
                ag_send(r, sign, u)

    node = lax.broadcasted_iota(jnp.int32, (rows, per), 0).astype(F32)

    def pick_block(y):
        pick = (node == idx_in[y][0:1, :]).astype(BF16)
        picks[y] = pick
        g = split(gath[0, at(y, rows), :])
        send_buf[y] = mm(pick, g[0], 0, 0) + mm(pick, g[1], 0, 0)
        there = at((my_x * NY + y) * 2 + core, cap)

        @pl.loop(1, na)
        def _(i):
            a = lax.rem(my_a + i, na)
            send(send_buf.at[y, at(a, cap)], recv_buf.at[there], sems.at[2], sems.at[3], a_dev(a))

        recv_buf[there, :] = send_buf[y, at(my_a, cap), :]

    pick_block(my_y)
    loads[4].wait()
    for j in range(blocks):
        hi, lo = split(t_ref[:, j * rows:(j + 1) * rows])
        th[j] = hi
        tl[j] = lo
    for c in loads[5:]:
        c.wait()
    feeds = lax.broadcasted_iota(jnp.int32, (rows, slots), 0) == dst_ref[...]
    s2 = tuple(
        jnp.where(feeds, jnp.broadcast_to(c.astype(F32), (rows, slots)), 0.0).astype(BF16)
        for c in split(cw_ref[...])
    )
    w2 = split(w_ref[...])

    def local_block(j):
        return mm3((th[j], tl[j]), split(gath[1, at(j, rows), :]))

    agg = local_block(me_b)
    wait_bytes(idx_in.at[pl.ds(0, n - 1)], sems.at[1])
    for d in (1, 2, 3):
        for h in (0, 1):
            u = 2 * (d - 1) + h
            for r in (0, 1):
                for sign in (1, -1):
                    ag_wait(r, sign, u)
                    if u < 5:
                        ag_send(r, sign, u + 2)
        pick_block(turn(0, d))
        pick_block(turn(0, -d))
        agg = agg + local_block(turn(1, d)) + local_block(turn(1, -d))
    for r in (0, 1):
        for sign in (1, -1):
            ag_wait(r, sign, 6)
    pick_block(turn(0, 4))
    agg = agg + local_block(turn(1, 4))

    wait_bytes(recv_buf.at[pl.ds(0, cap * n * (na - 1))], sems.at[3])
    agg = agg + mm3(s2, split(recv_buf[...]))
    agg2 = split(agg)
    pre = mm3(agg2, w2)
    cdf = 0.5 * (1.0 + lax.erf(pre * 0.7071067811865476))
    out_ref[...] = pre * cdf
    slope = cdf + pre * (jnp.exp(-0.5 * pre * pre) * 0.3989422804014327)
    gp2 = split(ct_ref[...] * slope)

    sp2 = split(mm3(gp2, w2, 1, 1))
    send2_buf[...] = mm3(s2, sp2, 0, 0)

    def give_back(y):
        @pl.loop(1, na)
        def _(i):
            a = lax.rem(my_a + i, na)
            p = ((a // 2) * NY + y) * 2 + lax.rem(a, 2)
            send(send2_buf.at[at(p, cap)], recv2_buf.at[y, at(my_a, cap)], sems.at[4], row_r.at[y], a_dev(a))

        recv2_buf[y, at(my_a, cap), :] = send2_buf[at((my_x * NY + y) * 2 + core, cap), :]

    for d in (4, 3, -3, 2, -2, 1, -1, 0):
        give_back(turn(0, d))

    wpart[...] = mm3(agg2, gp2, 0, 0)
    wrows = wpart.shape[0] // blocks

    @pl.loop(1, blocks)
    def _(i):
        j = turn(1, i)
        send(wpart.at[at(j, wrows)], wz.at[me_b], sems.at[6], sems.at[7], z_dev(j))

    wz[me_b] = wpart[at(me_b, wrows), :]

    for j in range(blocks):
        part[1, j] = mm3((th[j], tl[j]), sp2, 0, 0)

    def boundary_block(y):
        wait_bytes(recv2_buf.at[y, pl.ds(0, cap * (na - 1))], row_r.at[y])
        b = split(recv2_buf[y])
        part[0, y] = mm(picks[y], b[0]) + mm(picks[y], b[1])

    def rs_half(sign, u):
        return (u % 2) if sign > 0 else (1 - u % 2)

    def rs_step(r, sign, u):
        k = 2 * r + (0 if sign > 0 else 1)
        owner = turn(r, sign * (4 - (u + 1) // 2))
        h = rs_half(sign, u) * unit
        v = part[r, owner, h:h + unit, :]
        if u >= 2:
            wait_bytes(rs_in.at[k, u - 2], rs_r.at[k * 7 + u - 2])
            v = v + rs_in[k, u - 2]
        rs_out[k, u] = v
        send(rs_out.at[k, u], rs_in.at[k, u], rs_s.at[k], rs_r.at[k * 7 + u], ring[r][1](turn(r, sign)))

    def rs_all(r, u):
        rs_step(r, 1, u)
        rs_step(r, -1, u)

    rs_all(1, 0)
    rs_all(1, 1)
    boundary_block(turn(0, 4))
    rs_all(0, 0)
    boundary_block(turn(0, 3))
    boundary_block(turn(0, -3))
    rs_all(0, 1)

    half = width // 2
    piece = 2 * wrows // na

    def weight_a():
        wait_bytes(wz.at[pl.ds(0, blocks - 1)], sems.at[7])
        total = jnp.sum(wz[...], axis=0)
        wsum[0:wrows, :] = total[:, :half]
        wsum[wrows:, :] = total[:, half:]

        @pl.loop(1, na)
        def _(i):
            a = lax.rem(my_a + i, na)
            send(wsum.at[at(a, piece)], wa.at[my_a], sems.at[8], sems.at[9], a_dev(a))

        wa[my_a] = wsum[at(my_a, piece), :]

    def weight_y():
        wait_bytes(wa.at[pl.ds(0, na - 1)], sems.at[9])
        wy[my_y] = jnp.sum(wa[...], axis=0)

        @pl.loop(1, n)
        def _(i):
            send(wy.at[my_y], wy.at[my_y], sems.at[10], sems.at[11], y_dev(turn(0, i)))

    def weight_back_a():
        wait_bytes(wy.at[pl.ds(0, n - 1)], sems.at[11])
        nodes = rows * groups * blocks
        wfin[my_a] = jnp.sum(wy[...], axis=0) * nodes ** (-0.5)

        @pl.loop(1, na)
        def _(i):
            send(wfin.at[my_a], wfin.at[my_a], sems.at[12], sems.at[13], a_dev(lax.rem(my_a + i, na)))

    def weight_back_z():
        wait_bytes(wfin.at[pl.ds(0, na - 1)], sems.at[13])
        wall[me_b] = wfin[...].reshape(na * piece, half)

        @pl.loop(1, blocks)
        def _(i):
            send(wall.at[me_b], wall.at[me_b], sems.at[14], sems.at[15], z_dev(turn(1, i)))

    rs_all(1, 2)
    rs_all(0, 2)
    weight_a()
    boundary_block(turn(0, 2))
    boundary_block(turn(0, -2))
    rs_all(1, 3)
    rs_all(0, 3)
    weight_y()
    rs_all(1, 4)
    rs_all(0, 4)
    weight_back_a()
    boundary_block(turn(0, 1))
    boundary_block(turn(0, -1))
    rs_all(1, 5)
    rs_all(0, 5)
    weight_back_z()
    rs_all(1, 6)
    rs_all(0, 6)
    boundary_block(my_y)

    for r in (0, 1):
        for u in (5, 6):
            for k in (2 * r, 2 * r + 1):
                wait_bytes(rs_in.at[k, u], rs_r.at[k * 7 + u])
    for h in (0, 1):
        own = part[0, my_y, h * unit:(h + 1) * unit, :] + part[1, me_b, h * unit:(h + 1) * unit, :]
        for r in (0, 1):
            own = own + (rs_in[2 * r, 6 - h] + rs_in[2 * r + 1, 5 + h])
        gf_ref[h * unit:(h + 1) * unit, :] = own

    wait_bytes(wall.at[pl.ds(0, blocks - 1)], sems.at[15])
    for j in range(blocks):
        gw_ref[j * wrows:(j + 1) * wrows, :half] = wall[j, 0:wrows, :]
        gw_ref[j * wrows:(j + 1) * wrows, half:] = wall[j, wrows:, :]

    for k in range(4):
        wait_bytes(gath.at[0, pl.ds(0, 7 * unit)], ag_s.at[k])
        wait_bytes(rs_out.at[k], rs_s.at[k])
    wait_bytes(idx_out.at[pl.ds(0, n - 1)], sems.at[0])
    wait_bytes(recv_buf.at[pl.ds(0, cap * n * (na - 1))], sems.at[2])
    wait_bytes(recv_buf.at[pl.ds(0, cap * n * (na - 1))], sems.at[4])
    wait_bytes(wz.at[pl.ds(0, blocks - 1)], sems.at[6])
    wait_bytes(wa.at[pl.ds(0, na - 1)], sems.at[8])
    wait_bytes(wy.at[pl.ds(0, n - 1)], sems.at[10])
    wait_bytes(wfin.at[pl.ds(0, na - 1)], sems.at[12])
    wait_bytes(wall.at[pl.ds(0, blocks - 1)], sems.at[14])


def body(features, tiles, weight, cotangent, send_count, send_index, cross_dst, cross_weight):
    rows, width = features.shape
    groups = lax.axis_size("comm")
    blocks = lax.axis_size("blk")
    slots = send_index.shape[1]
    cap = slots // groups
    na = groups // NY
    per = na * cap
    unit = rows // 2
    wrows = width // blocks
    piece = 2 * wrows // na
    half = width // 2
    vmem = pltpu.VMEM
    dma = pltpu.SemaphoreType.DMA
    return pl.pallas_call(
        functools.partial(kernel, groups, blocks),
        out_shape=(
            jax.ShapeDtypeStruct((rows, width), F32),
            jax.ShapeDtypeStruct((rows, width), F32),
            jax.ShapeDtypeStruct((width, width), F32),
        ),
        in_specs=[pl.BlockSpec(memory_space=pltpu.HBM)] * 8,
        out_specs=(pl.BlockSpec(memory_space=vmem),) * 3,
        scratch_shapes=[
            vmem(tiles.shape, F32), vmem(weight.shape, F32), vmem((rows, width), F32),
            vmem(send_count.shape, jnp.int32), vmem(send_index.shape, jnp.int32),
            vmem(cross_dst.shape, jnp.int32), vmem(cross_weight.shape, F32),
            vmem((2, NY * rows, width), F32),
            vmem((NY, rows, per), BF16),
            vmem((blocks, rows, rows), BF16), vmem((blocks, rows, rows), BF16),
            vmem((NY, 8, per), F32), vmem((NY, 8, per), F32),
            vmem((NY, per, width), F32), vmem((slots, width), F32),
            vmem((slots, width), F32), vmem((NY, per, width), F32),
            vmem((2, NY, rows, width), F32),
            vmem((4, 7, unit, width), F32), vmem((4, 7, unit, width), F32),
            vmem((width, width), F32),
            vmem((blocks, wrows, width), F32),
            vmem((na, piece, half), F32),
            vmem((NY, piece, half), F32),
            vmem((na, piece, half), F32),
            vmem((blocks, 2 * wrows, half), F32),
            vmem((2 * wrows, half), F32),
            dma((9,)), dma((28,)), dma((4,)), dma((28,)), dma((4,)), dma((NY,)), dma((16,)),
        ],
        compiler_params=pltpu.CompilerParams(
            collective_id=0, has_side_effects=True, vmem_limit_bytes=60 * 1024 * 1024
        ),
    )(features, tiles, weight, cotangent, send_count, send_index, cross_dst, cross_weight)


def solution(mesh):
    rows = P(("comm", "blk"), None)
    return jax.shard_map(
        body,
        mesh=mesh,
        in_specs=(rows, rows, P(), rows, rows, rows, rows, rows),
        out_specs=(rows, rows, P()),
        check_vma=False,
    )
```

time: 394 us -> 76.9 us (0.20); the launches traced: 389 us -> 76.8 us
  waiting for transfers between devices: 312 us -> 0 us
  Pallas kernels: 0 us -> 73.2 us
  starting transfers between devices: 26 us -> 0 us
  other arithmetic: 18.9 us -> 0 us
  between operations: 13.9 us -> 0.66 us
  local copies, waits for them, and re-layouts: 11.1 us -> 2.98 us
  matrix products: 6.58 us -> 0 us
    psum x1 -> x0, waiting for transfers between devices: 252 us -> none  [body(): grad_weight = lax.psum(partial_weight, ('comm', 'blk')) * nodes ** (-0.5)]
    pallas_call x0 -> x1, Pallas kernels: none -> 73.2 us  [body(): pl.pallas_call(functools.partial(kernel, groups, blocks), out_shape=(jax....]
    reduce_scatter x1 -> x0, waiting for transfers between devices: 34.5 us -> none  [body(): lax.psum_scatter(lax.dot_general(columns, spread, (((0,), (0,)), ((), ())...]
    all_to_all x2 -> x0, starting transfers between devices: 25.9 us -> none  [the longest x1 14.2 us: body(): lax.all_to_all(slot_grads, 'comm', split_axis=0, concat_axis=0, tiled=True)]
    all_gather x1 -> x0, waiting for transfers between devices: 24.3 us -> none  [body(): lax.all_gather(features, 'blk', axis=0, tiled=True)]
    scatter-add x2 -> x0, other arithmetic: 12.3 us -> none  [the longest x1 6.13 us: body(): jax.ops.segment_sum(edge_weight[:, None] * incoming, targets, num_segment...]
    gather x2 -> x0, local copies, waits for them, and re-layouts: 6.93 us -> none  [the longest x1 3.47 us: body(): spread[targets]]
    dot_general x5 -> x0, matrix products: 6.58 us -> none  [the longest x1 2.01 us: body(): lax.dot_general(columns, spread, (((0,), (0,)), ((), ())), precision=high...]
  transfers between devices with their start and end apart: 5 -> 0, of which waited for: 4 -> 0; matrix products, arithmetic and copies ran while one was open for 5% -> 0% of each run, Pallas kernels for 0% -> 0%
where the time goes in v2:
time: 76.9 us; the launch traced here: 76.8 us
  Pallas kernels  73.2 us (95%)
  local copies, waits for them, and re-layouts  2.98 us (4%)
    pallas_call x1, Pallas kernels, body(): pl.pallas_call(functools.partial(kernel, groups, blocks), out_shape=(jax....  73.2 us
    unnamed x7, local copies, waits for them, and re-layouts  2.98 us

profile of v2, /device:TPU:1, one launch (start us, length us, event | category | flops | bytes accessed | tf_op | source)
XLA Modules:
  0.0 76.8 jit_solution(14270711335840979463)
XLA Ops:
  0.6 73.2 %shard_map.103 = (f32[128,256]{1,0:T(8,128)}, f32[128,256]{1,0:T(8,128)}, f32[256,256]{1,0:T(8,128)}) custom-call(f32[128,256]{1,0:T(8,128)} %f_hbm.1, f32[128,1024]{1,0:T(8,128)} %t_hbm.1, f32[256,256]{1,0:T(8,128)} %w_hbm.1, f32[128,256]{1,0:T(8,128)} %ct_hbm.1, s32[1,64]{1,0:T(1,128)} %cnt_hbm.1, s32[1,1024]{1,0:T(1,128)} %idx_hbm.1, s32[1,1024]{1,0:T(1,128)} %dst_hbm.1, ...), custom_call_target="tpu_custom_call" | custom-call | tf_op jit(solution)/shard_map/pallas_call | solution.py:373
  73.8 0.0 copy-start.1
  73.8 0.0 copy-start
  73.8 1.6 %copy.14 = f32[128,256]{1,0:T(8,128)} copy(f32[128,256]{1,0:T(8,128)} %get-tuple-element.6) | data formatting | bytes 262144
  75.4 0.0 copy-done.1
  75.4 0.7 copy.15
  76.1 0.0 copy-done
  76.1 0.7 copy.16
Async XLA Ops:
  73.8 1.6 %copy-start.1 = (f32[128,256]{1,0:T(8,128)S(1)}, f32[128,256]{1,0:T(8,128)}, u32[]{:S(2)}) copy-start(f32[128,256]{1,0:T(8,128)} %get-tuple-element.7) | copy-start | bytes 393220
  73.8 2.3 %copy-start = (f32[256,256]{1,0:T(8,128)S(1)}, f32[256,256]{1,0:T(8,128)}, u32[]{:S(2)}) copy-start(f32[256,256]{1,0:T(8,128)} %get-tuple-element.8) | copy-start | bytes 786436

commit v3 on v2

v3 whole, which is shorter than its diff:
```python
import functools

import jax
import jax.numpy as jnp
from jax import lax
from jax.experimental import pallas as pl
from jax.experimental.pallas import tpu as pltpu
from jax.sharding import PartitionSpec as P

MESH = pl.DeviceIdType.MESH
F32 = jnp.float32
BF16 = jnp.bfloat16
NY = 8
PARTS = 4
UNITS = 7 * PARTS // 2


def split(x):
    hi = x.astype(BF16)
    lo = (x - hi.astype(F32)).astype(BF16)
    return hi, lo


def mm(a, b, ca=1, cb=0):
    return lax.dot_general(a, b, (((ca,), (cb,)), ((), ())), preferred_element_type=F32)


def left(x, axis=1):
    return jnp.concatenate((x[0], x[0], x[1]), axis=axis)


def right(x):
    return jnp.concatenate((x[0], x[1], x[0]), axis=0)


def at(i, n):
    return pl.ds(pl.multiple_of(i * n, n), n)


def kernel(
    groups, blocks,
    f_hbm, t_hbm, w_hbm, ct_hbm, cnt_hbm, idx_hbm, dst_hbm, cw_hbm,
    out_ref, gf_ref, gw_ref,
    t_ref, w_ref, ct_ref, cnt_ref, idx_ref, dst_ref, cw_ref,
    gath, picks, t3, tt3, s3, st3, w3, wt3, idx_out, idx_in,
    send_buf, recv_buf, send2_buf, recv2_buf, part, rs_out, rs_in,
    wpart, wz, wa, wy, wfin, wall, wsum,
    loc, ag_r, ag_s, rs_r, rs_s, row_r, rowf_r, sems,
):
    rows, width = f_hbm.shape
    slots = idx_ref.shape[1]
    cap = slots // groups
    na = groups // NY
    unit = rows // PARTS
    me_c = lax.axis_index("comm")
    me_b = lax.axis_index("blk")
    core = lax.rem(me_c, 2)
    my_y = lax.rem(me_c // 2, NY)
    my_x = me_c // (2 * NY)
    my_a = my_x * 2 + core

    def a_dev(a):
        return (((a // 2) * NY + my_y) * 2 + lax.rem(a, 2), me_b)

    def y_dev(y):
        return ((my_x * NY + y) * 2 + core, me_b)

    def z_dev(z):
        return (me_c, z)

    ring = ((my_y, y_dev), (me_b, z_dev))
    n = NY

    def turn(r, d):
        return lax.rem(ring[r][0] + d + n, n)

    def send(src, dst, s, r, dev):
        pltpu.make_async_remote_copy(
            src_ref=src, dst_ref=dst, send_sem=s, recv_sem=r,
            device_id=dev, device_id_type=MESH,
        ).start()

    def wait_bytes(ref, s):
        pltpu.make_async_copy(ref, ref, s).wait()

    loads = [
        pltpu.make_async_copy(src, dst, loc.at[i])
        for i, (src, dst) in enumerate((
            (idx_hbm, idx_ref), (cnt_hbm, cnt_ref),
            (f_hbm, gath.at[0, at(my_y, rows)]), (f_hbm, gath.at[1, at(me_b, rows)]),
            (t_hbm, t_ref), (dst_hbm, dst_ref), (cw_hbm, cw_ref), (w_hbm, w_ref), (ct_hbm, ct_ref),
        ))
    ]
    for c in loads:
        c.start()

    barrier = pltpu.get_barrier_semaphore()

    @pl.loop(1, n)
    def _(i):
        pl.semaphore_signal(barrier, inc=1, device_id=y_dev(turn(0, i)), device_id_type=MESH)
        pl.semaphore_signal(barrier, inc=1, device_id=z_dev(turn(1, i)), device_id_type=MESH)
        pl.semaphore_signal(barrier, inc=1, device_id=a_dev(lax.rem(my_a + i, na)), device_id_type=MESH)

    loads[2].wait()
    loads[3].wait()

    pl.semaphore_wait(barrier, 3 * (n - 1))

    def part_of(sign, u):
        return (u % PARTS) if sign > 0 else (PARTS - 1 - u % PARTS)

    def ring_no(r, sign):
        return 2 * r + (0 if sign > 0 else 1)

    def ag_slice(r, sign, u, origin):
        return gath.at[r, pl.ds(pl.multiple_of(origin * rows + part_of(sign, u) * unit, unit), unit)]

    def ag_send(r, sign, u):
        s = ag_slice(r, sign, u, turn(r, -sign * (u // PARTS)))
        k = ring_no(r, sign)
        send(s, s, ag_s.at[k], ag_r.at[k * UNITS + u], ring[r][1](turn(r, sign)))

    def ag_wait(r, sign, u):
        s = ag_slice(r, sign, u, turn(r, -sign * (u // PARTS + 1)))
        wait_bytes(s, ag_r.at[ring_no(r, sign) * UNITS + u])

    for u in range(PARTS):
        for r in (0, 1):
            for sign in (1, -1):
                ag_send(r, sign, u)

    per = na * cap
    spot = lax.broadcasted_iota(jnp.int32, (groups, slots), 1) // cap
    peer = lax.broadcasted_iota(jnp.int32, (groups, slots), 0)
    expand = (spot == peer).astype(BF16)
    lane = lax.broadcasted_iota(jnp.int32, (16, slots), 1)
    row16 = lax.broadcasted_iota(jnp.int32, (16, slots), 0)
    here = (lane // (2 * cap)) % NY == row16
    source = lax.broadcasted_iota(jnp.int32, (slots, per), 0)
    target = lax.broadcasted_iota(jnp.int32, (slots, per), 1)
    gather_lane = ((source // (2 * cap * NY)) * (2 * cap) + source % (2 * cap) == target).astype(BF16)
    place = lax.rem(lane, cap).astype(F32)

    def by_y(v):
        v = jnp.broadcast_to(v, (16, slots)).astype(F32)
        return mm(jnp.where(here, v, 0.0).astype(BF16), gather_lane)

    loads[0].wait()
    loads[1].wait()
    counts = jnp.broadcast_to(cnt_ref[...].astype(F32).astype(BF16), (16, groups))
    count = mm(counts, expand)
    index = jnp.where(place < count, jnp.broadcast_to(idx_ref[...], (16, slots)).astype(F32), -1.0)
    mine = by_y(index)
    for y in range(NY):
        idx_out[y] = jnp.broadcast_to(mine[y:y + 1, :], (8, per))
    idx_in[my_y] = idx_out[my_y]

    @pl.loop(1, n)
    def _(i):
        y = turn(0, i)
        send(idx_out.at[y], idx_in.at[my_y], sems.at[0], sems.at[1], y_dev(y))

    node = lax.broadcasted_iota(jnp.int32, (rows, per), 0).astype(F32)

    def pick_block(y):
        pick = (node == idx_in[y][0:1, :]).astype(F32)
        one = pick.astype(BF16)
        picks[y] = jnp.concatenate((one, one), axis=1)
        flip = pick.T.astype(BF16)
        g = split(gath[0, at(y, rows), :])
        send_buf[y] = mm(jnp.concatenate((flip, flip), axis=1), jnp.concatenate(g, axis=0))

        @pl.loop(1, na)
        def _(i):
            a = lax.rem(my_a + i, na)
            send(send_buf.at[y, at(a, cap)], recv_buf.at[y, at(my_a, cap)], sems.at[2], rowf_r.at[y], a_dev(a))

        recv_buf[y, at(my_a, cap), :] = send_buf[y, at(my_a, cap), :]

    def make_tiles(js):
        for j in js:
            v = t_ref[:, j * rows:(j + 1) * rows]
            t3[j] = left(split(v))
            tt3[j] = left(split(v.T))

    def cross_wait(y):
        wait_bytes(recv_buf.at[y, pl.ds(0, cap * (na - 1))], rowf_r.at[y])

    def gathered(ref, blocks_of, data):
        a = jnp.concatenate([ref[b] for b in blocks_of], axis=1)
        return mm(a, jnp.concatenate([right(split(data(b))) for b in blocks_of], axis=0))

    def local_blocks(*js):
        return gathered(t3, js, lambda j: gath[1, at(j, rows), :])

    def cross_blocks(*ys):
        for y in ys:
            cross_wait(y)
        return gathered(s3, ys, lambda y: recv_buf[y])

    def ring_step(k):
        for u in range(k * PARTS // 2, (k + 1) * PARTS // 2):
            for r in (0, 1):
                for sign in (1, -1):
                    ag_wait(r, sign, u)
                    if u + PARTS < UNITS:
                        ag_send(r, sign, u + PARTS)

    pick_block(my_y)
    ring_step(0)
    for c in loads[4:]:
        c.wait()
    make_tiles(range(blocks))
    wait_bytes(idx_in.at[pl.ds(0, n - 1)], sems.at[1])
    ring_step(1)
    pick_block(turn(0, 1))
    pick_block(turn(0, -1))
    ring_step(2)
    feed = by_y(dst_ref[...])
    cw2 = split(cw_ref[...])
    weight_hi = by_y(cw2[0].astype(F32))
    weight_lo = by_y(cw2[1].astype(F32))
    for y in range(NY):
        hit = node == feed[y:y + 1, :]
        hi = jnp.where(hit, jnp.broadcast_to(weight_hi[y:y + 1, :], (rows, per)), 0.0)
        lo = jnp.where(hit, jnp.broadcast_to(weight_lo[y:y + 1, :], (rows, per)), 0.0)
        s3[y] = left((hi.astype(BF16), lo.astype(BF16)))
        st3[y] = left((hi.T.astype(BF16), lo.T.astype(BF16)))
    ring_step(3)
    pick_block(turn(0, 2))
    pick_block(turn(0, -2))
    ring_step(4)
    w3[...] = right(split(w_ref[...]))
    wt3[...] = right(split(w_ref[...].T))
    agg = local_blocks(me_b, turn(1, 1), turn(1, -1))
    ring_step(5)
    pick_block(turn(0, 3))
    pick_block(turn(0, -3))
    ring_step(6)
    pick_block(turn(0, 4))
    agg = agg + local_blocks(turn(1, 2), turn(1, -2))
    agg = agg + local_blocks(turn(1, 3), turn(1, -3), turn(1, 4))
    agg = agg + cross_blocks(my_y, turn(0, 1), turn(0, -1))
    agg = agg + cross_blocks(turn(0, 2), turn(0, -2))
    agg = agg + cross_blocks(turn(0, 3), turn(0, -3), turn(0, 4))
    agg2 = split(agg)
    pre = mm(left(agg2), w3[...])
    cdf = 0.5 * (1.0 + lax.erf(pre * 0.7071067811865476))
    out_ref[...] = pre * cdf
    slope = cdf + pre * (jnp.exp(-0.5 * pre * pre) * 0.3989422804014327)
    gp2 = split(ct_ref[...] * slope)

    sp3 = right(split(mm(left(gp2), wt3[...])))

    def give_back(y):
        send2_buf[y] = mm(st3[y], sp3)

        @pl.loop(1, na)
        def _(i):
            a = lax.rem(my_a + i, na)
            send(send2_buf.at[y, at(a, cap)], recv2_buf.at[y, at(my_a, cap)], sems.at[4], row_r.at[y], a_dev(a))

        recv2_buf[y, at(my_a, cap), :] = send2_buf[y, at(my_a, cap), :]

    def inner_block(j):
        part[1, j] = mm(tt3[j], sp3)

    def boundary_block(y):
        wait_bytes(recv2_buf.at[y, pl.ds(0, cap * (na - 1))], row_r.at[y])
        part[0, y] = mm(picks[y], jnp.concatenate(split(recv2_buf[y]), axis=0))

    def rs_step(r, sign, u):
        k = ring_no(r, sign)
        owner = turn(r, sign * (4 - (u + PARTS // 2) // PARTS))
        h = part_of(sign, u) * unit
        v = part[r, owner, h:h + unit, :]
        if u >= PARTS:
            wait_bytes(rs_in.at[k, u - PARTS], rs_r.at[k * UNITS + u - PARTS])
            v = v + rs_in[k, u - PARTS]
        rs_out[k, u] = v
        send(rs_out.at[k, u], rs_in.at[k, u], rs_s.at[k], rs_r.at[k * UNITS + u], ring[r][1](turn(r, sign)))

    def rs_all(r, k):
        for u in range(k * PARTS // 2, (k + 1) * PARTS // 2):
            rs_step(r, 1, u)
            rs_step(r, -1, u)

    wrows = width // na
    half = width // 2
    piece = 2 * wrows // n

    def weight_1():
        wpart[...] = mm(left(agg2, 0), right(gp2), 0, 0)

        @pl.loop(1, na)
        def _(i):
            a = lax.rem(my_a + i, na)
            send(wpart.at[at(a, wrows)], wz.at[my_a], sems.at[6], sems.at[7], a_dev(a))

        wz[my_a] = wpart[at(my_a, wrows), :]

    def weight_2():
        wait_bytes(wz.at[pl.ds(0, na - 1)], sems.at[7])
        total = jnp.sum(wz[...], axis=0)
        wsum[0:wrows, :] = total[:, :half]
        wsum[wrows:, :] = total[:, half:]

        @pl.loop(1, n)
        def _(i):
            y = turn(0, i)
            send(wsum.at[at(y, piece)], wa.at[my_y], sems.at[8], sems.at[9], y_dev(y))

        wa[my_y] = wsum[at(my_y, piece), :]

    def weight_3():
        wait_bytes(wa.at[pl.ds(0, n - 1)], sems.at[9])
        wy[me_b] = jnp.sum(wa[...], axis=0)

        @pl.loop(1, n)
        def _(i):
            send(wy.at[me_b], wy.at[me_b], sems.at[10], sems.at[11], z_dev(turn(1, i)))

    def weight_4():
        wait_bytes(wy.at[pl.ds(0, n - 1)], sems.at[11])
        nodes = rows * groups * blocks
        wfin[my_y] = jnp.sum(wy[...], axis=0) * nodes ** (-0.5)

        @pl.loop(1, n)
        def _(i):
            send(wfin.at[my_y], wfin.at[my_y], sems.at[12], sems.at[13], y_dev(turn(0, i)))

    def weight_5():
        wait_bytes(wfin.at[pl.ds(0, n - 1)], sems.at[13])
        wall[my_a] = wfin[...].reshape(n * piece, half)

        @pl.loop(1, na)
        def _(i):
            send(wall.at[my_a], wall.at[my_a], sems.at[14], sems.at[15], a_dev(lax.rem(my_a + i, na)))

    weight_1()
    inner_block(turn(1, 4))
    rs_all(1, 0)
    inner_block(turn(1, 3))
    inner_block(turn(1, -3))
    rs_all(1, 1)
    for d in (4, 3, -3, 2, -2, 1, -1, 0):
        give_back(turn(0, d))
    inner_block(turn(1, 2))
    inner_block(turn(1, -2))
    rs_all(1, 2)
    weight_2()
    boundary_block(turn(0, 4))
    rs_all(0, 0)
    boundary_block(turn(0, 3))
    boundary_block(turn(0, -3))
    rs_all(0, 1)
    rs_all(1, 3)
    inner_block(turn(1, 1))
    inner_block(turn(1, -1))
    weight_3()
    rs_all(1, 4)
    rs_all(0, 2)
    boundary_block(turn(0, 2))
    boundary_block(turn(0, -2))
    rs_all(0, 3)
    weight_4()
    rs_all(1, 5)
    rs_all(0, 4)
    boundary_block(turn(0, 1))
    boundary_block(turn(0, -1))
    rs_all(0, 5)
    rs_all(1, 6)
    weight_5()
    rs_all(0, 6)
    inner_block(me_b)
    boundary_block(my_y)

    last = range(UNITS - PARTS, UNITS)
    for k in range(4):
        for u in last:
            wait_bytes(rs_in.at[k, u], rs_r.at[k * UNITS + u])
    for h in range(PARTS):
        at_h = slice(h * unit, (h + 1) * unit)
        own = part[0, my_y, at_h, :] + part[1, me_b, at_h, :]
        for r in (0, 1):
            for sign in (1, -1):
                for u in last:
                    if part_of(sign, u) == h:
                        own = own + rs_in[ring_no(r, sign), u]
        gf_ref[at_h, :] = own

    wait_bytes(wall.at[pl.ds(0, na - 1)], sems.at[15])
    for j in range(na):
        gw_ref[j * wrows:(j + 1) * wrows, :half] = wall[j, 0:wrows, :]
        gw_ref[j * wrows:(j + 1) * wrows, half:] = wall[j, wrows:, :]

    for k in range(4):
        wait_bytes(gath.at[0, pl.ds(0, UNITS * unit)], ag_s.at[k])
        wait_bytes(rs_out.at[k], rs_s.at[k])
    wait_bytes(idx_out.at[pl.ds(0, n - 1)], sems.at[0])
    wait_bytes(recv_buf.at[pl.ds(0, n - 1)], sems.at[2])
    wait_bytes(recv_buf.at[pl.ds(0, n - 1)], sems.at[4])
    wait_bytes(wz.at[pl.ds(0, blocks - 1)], sems.at[6])
    wait_bytes(wa.at[pl.ds(0, na - 1)], sems.at[8])
    wait_bytes(wy.at[pl.ds(0, n - 1)], sems.at[10])
    wait_bytes(wfin.at[pl.ds(0, na - 1)], sems.at[12])
    wait_bytes(wall.at[pl.ds(0, blocks - 1)], sems.at[14])


def body(features, tiles, weight, cotangent, send_count, send_index, cross_dst, cross_weight):
    rows, width = features.shape
    groups = lax.axis_size("comm")
    blocks = lax.axis_size("blk")
    slots = send_index.shape[1]
    cap = slots // groups
    na = groups // NY
    per = na * cap
    unit = rows // PARTS
    wrows = width // blocks
    piece = 2 * wrows // na
    half = width // 2
    vmem = pltpu.VMEM
    dma = pltpu.SemaphoreType.DMA
    return pl.pallas_call(
        functools.partial(kernel, groups, blocks),
        out_shape=(
            jax.ShapeDtypeStruct((rows, width), F32),
            jax.ShapeDtypeStruct((rows, width), F32),
            jax.ShapeDtypeStruct((width, width), F32),
        ),
        in_specs=[pl.BlockSpec(memory_space=pltpu.HBM)] * 8,
        out_specs=(pl.BlockSpec(memory_space=vmem),) * 3,
        scratch_shapes=[
            vmem(tiles.shape, F32), vmem(weight.shape, F32), vmem((rows, width), F32),
            vmem(send_count.shape, jnp.int32), vmem(send_index.shape, jnp.int32),
            vmem(cross_dst.shape, jnp.int32), vmem(cross_weight.shape, F32),
            vmem((2, NY * rows, width), F32),
            vmem((NY, rows, 2 * per), BF16),
            vmem((blocks, rows, 3 * rows), BF16), vmem((blocks, rows, 3 * rows), BF16),
            vmem((NY, rows, 3 * per), BF16), vmem((NY, per, 3 * rows), BF16),
            vmem((3 * width, width), BF16), vmem((3 * width, width), BF16),
            vmem((NY, 8, per), F32), vmem((NY, 8, per), F32),
            vmem((NY, per, width), F32), vmem((NY, per, width), F32),
            vmem((NY, per, width), F32), vmem((NY, per, width), F32),
            vmem((2, NY, rows, width), F32),
            vmem((4, UNITS, unit, width), F32), vmem((4, UNITS, unit, width), F32),
            vmem((width, width), F32),
            vmem((blocks, wrows, width), F32),
            vmem((na, piece, half), F32),
            vmem((NY, piece, half), F32),
            vmem((na, piece, half), F32),
            vmem((blocks, 2 * wrows, half), F32),
            vmem((2 * wrows, half), F32),
            dma((9,)), dma((4 * UNITS,)), dma((4,)), dma((4 * UNITS,)), dma((4,)), dma((NY,)), dma((NY,)), dma((16,)),
        ],
        compiler_params=pltpu.CompilerParams(
            collective_id=0, has_side_effects=True, vmem_limit_bytes=48 * 1024 * 1024
        ),
    )(*(pltpu.with_memory_space_constraint(v, pltpu.HBM) for v in (
        features, tiles, weight, cotangent, send_count, send_index, cross_dst, cross_weight)))


def solution(mesh):
    rows = P(("comm", "blk"), None)
    return jax.shard_map(
        body,
        mesh=mesh,
        in_specs=(rows, rows, P(), rows, rows, rows, rows, rows),
        out_specs=(rows, rows, P()),
        check_vma=False,
    )
```

time: 76.9 us -> 67.9 us (0.88)
  Pallas kernels: 73.2 us -> 65.1 us
  local copies, waits for them, and re-layouts: 2.98 us -> 2.01 us
    pallas_call x1, Pallas kernels: 73.2 us -> 65.1 us  [body(): pl.pallas_call(functools.partial(kernel, groups, blocks), out_shape=(jax....]
    unnamed x7 -> x3, local copies, waits for them, and re-layouts: 2.98 us -> 2.01 us
where the time goes in v3:
time: 67.9 us; the launch traced here: 67.7 us
  Pallas kernels  65.1 us (96%)
  local copies, waits for them, and re-layouts  2.01 us (3%)
    pallas_call x1, Pallas kernels, body(): pl.pallas_call(functools.partial(kernel, groups, blocks), out_shape=(jax....  65.1 us
    unnamed x3, local copies, waits for them, and re-layouts  2.01 us

profile of v3, /device:TPU:1, one launch (start us, length us, event | category | flops | bytes accessed | tf_op | source)
XLA Modules:
  0.0 67.7 jit_solution(14546070208985896621)
XLA Ops:
  0.6 65.1 %shard_map.103 = (f32[128,256]{1,0:T(8,128)S(1)}, f32[128,256]{1,0:T(8,128)S(1)}, f32[256,256]{1,0:T(8,128)S(1)}) custom-call(f32[128,256]{1,0:T(8,128)} %f_hbm.1, f32[128,1024]{1,0:T(8,128)} %t_hbm.1, f32[256,256]{1,0:T(8,128)} %w_hbm.1, f32[128,256]{1,0:T(8,128)} %ct_hbm.1, s32[1,64]{1,0:T(1,128)} %cnt_hbm.1, s32[1,1024]{1,0:T(1,128)} %idx_hbm.1, ...), custom_call_target="tpu_custom_call" | custom-call | tf_op jit(solution)/shard_map/pallas_call | solution.py:425
  65.7 0.7 copy.14
  66.4 0.7 copy.15
  67.0 0.7 %copy.16 = f32[256,256]{1,0:T(8,128)} copy(f32[256,256]{1,0:T(8,128)S(1)} %get-tuple-element.8) | data formatting | bytes 524288

commit v4 on v3

--- a/solution.py
+++ b/solution.py
@@ -40,14 +40,17 @@
 def kernel(
     groups, blocks,
     f_hbm, t_hbm, w_hbm, ct_hbm, cnt_hbm, idx_hbm, dst_hbm, cw_hbm,
-    out_ref, gf_ref, gw_ref,
+    all_ref,
     t_ref, w_ref, ct_ref, cnt_ref, idx_ref, dst_ref, cw_ref,
     gath, picks, t3, tt3, s3, st3, w3, wt3, idx_out, idx_in,
     send_buf, recv_buf, send2_buf, recv2_buf, part, rs_out, rs_in,
     wpart, wz, wa, wy, wfin, wall, wsum,
-    loc, ag_r, ag_s, rs_r, rs_s, row_r, rowf_r, sems,
+    loc, ag_r, ag_s, rs_r, rs_s, row_r, rowf_r, wfin_r, sems,
 ):
     rows, width = f_hbm.shape
+    out_ref = all_ref.at[pl.ds(0, rows)]
+    gf_ref = all_ref.at[pl.ds(rows, rows)]
+    gw_ref = all_ref.at[pl.ds(2 * rows, width)]
     slots = idx_ref.shape[1]
     cap = slots // groups
     na = groups // NY
@@ -328,15 +331,19 @@
 
         @pl.loop(1, n)
         def _(i):
-            send(wfin.at[my_y], wfin.at[my_y], sems.at[12], sems.at[13], y_dev(turn(0, i)))
+            send(wfin.at[my_y], wfin.at[my_y], sems.at[12], wfin_r.at[my_y], y_dev(turn(0, i)))
 
     def weight_5():
-        wait_bytes(wfin.at[pl.ds(0, n - 1)], sems.at[13])
-        wall[my_a] = wfin[...].reshape(n * piece, half)
-
-        @pl.loop(1, na)
-        def _(i):
-            send(wall.at[my_a], wall.at[my_a], sems.at[14], sems.at[15], a_dev(lax.rem(my_a + i, na)))
+        for d in (0, 1, -1, 2, -2, 3, -3, 4):
+            y = turn(0, d)
+            if d:
+                wait_bytes(wfin.at[y], wfin_r.at[y])
+
+            @pl.loop(1, na)
+            def _(i):
+                send(wfin.at[y], wall.at[my_a, y], sems.at[14], sems.at[15], a_dev(lax.rem(my_a + i, na)))
+
+        wall[my_a] = wfin[...]
 
     weight_1()
     inner_block(turn(1, 4))
@@ -392,8 +399,8 @@
 
     wait_bytes(wall.at[pl.ds(0, na - 1)], sems.at[15])
     for j in range(na):
-        gw_ref[j * wrows:(j + 1) * wrows, :half] = wall[j, 0:wrows, :]
-        gw_ref[j * wrows:(j + 1) * wrows, half:] = wall[j, wrows:, :]
+        gw_ref[j * wrows:(j + 1) * wrows, :half] = wall[j, 0:n // 2].reshape(wrows, half)
+        gw_ref[j * wrows:(j + 1) * wrows, half:] = wall[j, n // 2:].reshape(wrows, half)
 
     for k in range(4):
         wait_bytes(gath.at[0, pl.ds(0, UNITS * unit)], ag_s.at[k])
@@ -405,7 +412,7 @@
     wait_bytes(wa.at[pl.ds(0, na - 1)], sems.at[8])
     wait_bytes(wy.at[pl.ds(0, n - 1)], sems.at[10])
     wait_bytes(wfin.at[pl.ds(0, na - 1)], sems.at[12])
-    wait_bytes(wall.at[pl.ds(0, blocks - 1)], sems.at[14])
+    wait_bytes(wall.at[pl.ds(0, na - 1)], sems.at[14])
 
 
 def body(features, tiles, weight, cotangent, send_count, send_index, cross_dst, cross_weight):
@@ -422,15 +429,11 @@
     half = width // 2
     vmem = pltpu.VMEM
     dma = pltpu.SemaphoreType.DMA
-    return pl.pallas_call(
+    full = pl.pallas_call(
         functools.partial(kernel, groups, blocks),
-        out_shape=(
-            jax.ShapeDtypeStruct((rows, width), F32),
-            jax.ShapeDtypeStruct((rows, width), F32),
-            jax.ShapeDtypeStruct((width, width), F32),
-        ),
+        out_shape=jax.ShapeDtypeStruct((2 * rows + width, width), F32),
         in_specs=[pl.BlockSpec(memory_space=pltpu.HBM)] * 8,
-        out_specs=(pl.BlockSpec(memory_space=vmem),) * 3,
+        out_specs=pl.BlockSpec(memory_space=vmem),
         scratch_shapes=[
             vmem(tiles.shape, F32), vmem(weight.shape, F32), vmem((rows, width), F32),
             vmem(send_count.shape, jnp.int32), vmem(send_index.shape, jnp.int32),
@@ -450,15 +453,17 @@
             vmem((na, piece, half), F32),
             vmem((NY, piece, half), F32),
             vmem((na, piece, half), F32),
-            vmem((blocks, 2 * wrows, half), F32),
+            vmem((na, NY, piece, half), F32),
             vmem((2 * wrows, half), F32),
-            dma((9,)), dma((4 * UNITS,)), dma((4,)), dma((4 * UNITS,)), dma((4,)), dma((NY,)), dma((NY,)), dma((16,)),
+            dma((9,)), dma((4 * UNITS,)), dma((4,)), dma((4 * UNITS,)), dma((4,)), dma((NY,)), dma((NY,)), dma((NY,)), dma((16,)),
         ],
         compiler_params=pltpu.CompilerParams(
             collective_id=0, has_side_effects=True, vmem_limit_bytes=48 * 1024 * 1024
         ),
     )(*(pltpu.with_memory_space_constraint(v, pltpu.HBM) for v in (
         features, tiles, weight, cotangent, send_count, send_index, cross_dst, cross_weight)))
+
+    return full[:rows], full[rows:2 * rows], full[2 * rows:]
 
 
 def solution(mesh):

time: 67.9 us -> 66.4 us (0.978)
  Pallas kernels: 65.1 us -> 64.2 us
    unnamed x3 -> x0, local copies, waits for them, and re-layouts: 2.01 us -> none
    slice x0 -> x2, local copies, waits for them, and re-layouts: none -> 1.44 us  [body(): return (full[:rows], full[rows:2 * rows], full[2 * rows:])]
    pallas_call x1, Pallas kernels: 65.1 us -> 64.2 us  [body(): pl.pallas_call(functools.partial(kernel, groups, blocks), out_shape=jax.S...]
where the time goes in v4:
time: 66.4 us; the launch traced here: 66.3 us
  Pallas kernels  64.2 us (97%)
  local copies, waits for them, and re-layouts  1.44 us (2%)
    pallas_call x1, Pallas kernels, body(): pl.pallas_call(functools.partial(kernel, groups, blocks), out_shape=jax.S...  64.2 us
    slice x2, local copies, waits for them, and re-layouts, body(): return (full[:rows], full[rows:2 * rows], full[2 * rows:])  1.44 us

profile of v4, /device:TPU:1, one launch (start us, length us, event | category | flops | bytes accessed | tf_op | source)
XLA Modules:
  0.0 66.3 jit_solution(14721560488527295784)
XLA Ops:
  0.6 64.2 %shard_map.103 = f32[512,256]{1,0:T(8,128)S(1)} custom-call(f32[128,256]{1,0:T(8,128)} %f_hbm.1, f32[128,1024]{1,0:T(8,128)} %t_hbm.1, f32[256,256]{1,0:T(8,128)} %w_hbm.1, f32[128,256]{1,0:T(8,128)} %ct_hbm.1, s32[1,64]{1,0:T(1,128)} %cnt_hbm.1, s32[1,1024]{1,0:T(1,128)} %idx_hbm.1, s32[1,1024]{1,0:T(1,128)} %dst_hbm.1, f32[1,1024]{1,0:T(1,128)} %cw_hbm.1), custom_call_target="tpu_custom_call" | custom-call | tf_op jit(solution)/shard_map/pallas_call | solution.py:432
  64.9 0.7 %fusion = (f32[128,256]{1,0:T(8,128)}, f32[128,256]{1,0:T(8,128)}) fusion(f32[512,256]{1,0:T(8,128)S(1)} %shard_map.103), kind=kLoop, calls=%fused_computation | loop fusion | bytes 524288 | tf_op jit(solution)/shard_map/slice | solution.py:466
  65.6 0.7 %slice.11 = f32[256,256]{1,0:T(8,128)} slice(f32[512,256]{1,0:T(8,128)S(1)} %shard_map.103), slice={[256:512], [0:256]} | slice | bytes 524288 | tf_op jit(solution)/shard_map/slice | solution.py:466

commit v5 on v4

--- a/solution.py
+++ b/solution.py
@@ -11,7 +11,7 @@
 F32 = jnp.float32
 BF16 = jnp.bfloat16
 NY = 8
-PARTS = 4
+PARTS = 2
 UNITS = 7 * PARTS // 2
 
 
@@ -42,7 +42,7 @@
     f_hbm, t_hbm, w_hbm, ct_hbm, cnt_hbm, idx_hbm, dst_hbm, cw_hbm,
     all_ref,
     t_ref, w_ref, ct_ref, cnt_ref, idx_ref, dst_ref, cw_ref,
-    gath, picks, t3, tt3, s3, st3, w3, wt3, idx_out, idx_in,
+    gath, picks, flips, t3, tt3, s3, st3, w3, wt3, idx_out, idx_in,
     send_buf, recv_buf, send2_buf, recv2_buf, part, rs_out, rs_in,
     wpart, wz, wa, wy, wfin, wall, wsum,
     loc, ag_r, ag_s, rs_r, rs_s, row_r, rowf_r, wfin_r, sems,
@@ -166,13 +166,16 @@
 
     node = lax.broadcasted_iota(jnp.int32, (rows, per), 0).astype(F32)
 
-    def pick_block(y):
+    def make_pick(y):
         pick = (node == idx_in[y][0:1, :]).astype(F32)
         one = pick.astype(BF16)
         picks[y] = jnp.concatenate((one, one), axis=1)
         flip = pick.T.astype(BF16)
+        flips[y] = jnp.concatenate((flip, flip), axis=1)
+
+    def pick_block(y):
         g = split(gath[0, at(y, rows), :])
-        send_buf[y] = mm(jnp.concatenate((flip, flip), axis=1), jnp.concatenate(g, axis=0))
+        send_buf[y] = mm(flips[y], jnp.concatenate(g, axis=0))
 
         @pl.loop(1, na)
         def _(i):
@@ -202,24 +205,31 @@
             cross_wait(y)
         return gathered(s3, ys, lambda y: recv_buf[y])
 
-    def ring_step(k):
+    def ring_step(r, k):
         for u in range(k * PARTS // 2, (k + 1) * PARTS // 2):
-            for r in (0, 1):
-                for sign in (1, -1):
-                    ag_wait(r, sign, u)
-                    if u + PARTS < UNITS:
-                        ag_send(r, sign, u + PARTS)
-
+            for sign in (1, -1):
+                ag_wait(r, sign, u)
+                if u + PARTS < UNITS:
+                    ag_send(r, sign, u + PARTS)
+
+    make_pick(my_y)
     pick_block(my_y)
-    ring_step(0)
+    ring_step(0, 0)
+    ring_step(1, 0)
     for c in loads[4:]:
         c.wait()
     make_tiles(range(blocks))
     wait_bytes(idx_in.at[pl.ds(0, n - 1)], sems.at[1])
-    ring_step(1)
+    for d in (1, -1):
+        make_pick(turn(0, d))
+    ring_step(0, 1)
     pick_block(turn(0, 1))
     pick_block(turn(0, -1))
-    ring_step(2)
+    ring_step(1, 1)
+    for d in (2, -2, 3, -3, 4):
+        make_pick(turn(0, d))
+    ring_step(0, 2)
+    ring_step(1, 2)
     feed = by_y(dst_ref[...])
     cw2 = split(cw_ref[...])
     weight_hi = by_y(cw2[0].astype(F32))
@@ -230,18 +240,22 @@
         lo = jnp.where(hit, jnp.broadcast_to(weight_lo[y:y + 1, :], (rows, per)), 0.0)
         s3[y] = left((hi.astype(BF16), lo.astype(BF16)))
         st3[y] = left((hi.T.astype(BF16), lo.T.astype(BF16)))
-    ring_step(3)
+    ring_step(0, 3)
     pick_block(turn(0, 2))
     pick_block(turn(0, -2))
-    ring_step(4)
+    ring_step(1, 3)
+    ring_step(0, 4)
+    ring_step(1, 4)
     w3[...] = right(split(w_ref[...]))
     wt3[...] = right(split(w_ref[...].T))
     agg = local_blocks(me_b, turn(1, 1), turn(1, -1))
-    ring_step(5)
+    ring_step(0, 5)
     pick_block(turn(0, 3))
     pick_block(turn(0, -3))
-    ring_step(6)
+    ring_step(1, 5)
+    ring_step(0, 6)
     pick_block(turn(0, 4))
+    ring_step(1, 6)
     agg = agg + local_blocks(turn(1, 2), turn(1, -2))
     agg = agg + local_blocks(turn(1, 3), turn(1, -3), turn(1, 4))
     agg = agg + cross_blocks(my_y, turn(0, 1), turn(0, -1))
@@ -365,9 +379,9 @@
     rs_all(1, 3)
     inner_block(turn(1, 1))
     inner_block(turn(1, -1))
+    rs_all(0, 2)
     weight_3()
     rs_all(1, 4)
-    rs_all(0, 2)
     boundary_block(turn(0, 2))
     boundary_block(turn(0, -2))
     rs_all(0, 3)
@@ -439,7 +453,7 @@
             vmem(send_count.shape, jnp.int32), vmem(send_index.shape, jnp.int32),
             vmem(cross_dst.shape, jnp.int32), vmem(cross_weight.shape, F32),
             vmem((2, NY * rows, width), F32),
-            vmem((NY, rows, 2 * per), BF16),
+            vmem((NY, rows, 2 * per), BF16), vmem((NY, per, 2 * rows), BF16),
             vmem((blocks, rows, 3 * rows), BF16), vmem((blocks, rows, 3 * rows), BF16),
             vmem((NY, rows, 3 * per), BF16), vmem((NY, per, 3 * rows), BF16),
             vmem((3 * width, width), BF16), vmem((3 * width, width), BF16),

time: 66.4 us -> 66 us (level)
  no operation moved by 1% of the time
where the time goes in v5:
time: 66 us; the launch traced here: 65.8 us
  Pallas kernels  63.7 us (97%)
  local copies, waits for them, and re-layouts  1.44 us (2%)
    pallas_call x1, Pallas kernels, body(): pl.pallas_call(functools.partial(kernel, groups, blocks), out_shape=jax.S...  63.7 us
    slice x2, local copies, waits for them, and re-layouts, body(): return (full[:rows], full[rows:2 * rows], full[2 * rows:])  1.44 us

profile of v5, /device:TPU:1, one launch (start us, length us, event | category | flops | bytes accessed | tf_op | source)
XLA Modules:
  0.0 65.8 jit_solution(1635513830803152345)
XLA Ops:
  0.6 63.7 %shard_map.103 = f32[512,256]{1,0:T(8,128)S(1)} custom-call(f32[128,256]{1,0:T(8,128)} %f_hbm.1, f32[128,1024]{1,0:T(8,128)} %t_hbm.1, f32[256,256]{1,0:T(8,128)} %w_hbm.1, f32[128,256]{1,0:T(8,128)} %ct_hbm.1, s32[1,64]{1,0:T(1,128)} %cnt_hbm.1, s32[1,1024]{1,0:T(1,128)} %idx_hbm.1, s32[1,1024]{1,0:T(1,128)} %dst_hbm.1, f32[1,1024]{1,0:T(1,128)} %cw_hbm.1), custom_call_target="tpu_custom_call" | custom-call | tf_op jit(solution)/shard_map/pallas_call | solution.py:446
  64.4 0.7 %fusion = (f32[128,256]{1,0:T(8,128)}, f32[128,256]{1,0:T(8,128)}) fusion(f32[512,256]{1,0:T(8,128)S(1)} %shard_map.103), kind=kLoop, calls=%fused_computation | loop fusion | bytes 524288 | tf_op jit(solution)/shard_map/slice | solution.py:480
  65.1 0.7 %slice.11 = f32[256,256]{1,0:T(8,128)} slice(f32[512,256]{1,0:T(8,128)S(1)} %shard_map.103), slice={[256:512], [0:256]} | slice | bytes 524288 | tf_op jit(solution)/shard_map/slice | solution.py:480
